TPU v7x, 1024 devices: a whole 4x8x16 slice. The times are simulated.
1024 devices in a mesh: node: 128 (over z_lo, y, core), local: 8 (over z_hi, x).
Axes of the slice: x: 4, y: 8, z: 16 (z_hi: 2, z_lo: 8; z = z_hi * 8 + z_lo), core: 2. Of those that a mesh axis runs over, the one named last changes fastest.
Arguments:
- tokens: bfloat16 [131072, 4096], P('node'), may hold values from -6 to 6
- hidden_grad: bfloat16 [131072, 768], P('node', 'local'), may hold values from -6 to 6
- master: float32 [2, 4096, 768], P(None, 'node', 'local'), may hold values from -0.09375 to 0.09375
- counts: int32 [1024], P(('node', 'local')), may hold values from 0 to 128, as said below
Outputs:
- hidden: bfloat16 [131072, 768], P('node', 'local')
- weight_grad: float32 [2, 4096, 768], P(None, 'node', 'local')
Inputs may be any that keep to these rules, and one draw needn't show every extreme that they name: `counts`: each count is a multiple of 16; some device is full in every draw.
All inputs are finite; a program needn't handle non-finite values.
Results may differ from a plain program's by a relative error of at most 0.0058.
Values may be sent and summed in bfloat16 or wider, within the bound.
A program may use at most 32 MiB of HBM per device.

v0:
```python
import jax
import jax.numpy as jnp
from jax import lax
from jax.sharding import PartitionSpec as P


def on_device(tokens, hidden_grad, master, counts):
    shard = master.astype(jnp.bfloat16)
    node_counts = lax.all_gather(counts, "local", axis=0, tiled=True)
    rows_node = tokens.shape[0]
    group_size = node_counts.shape[0]
    rows_dev = rows_node // group_size
    position = jnp.arange(rows_node, dtype=jnp.int32) % rows_dev
    limits = jnp.broadcast_to(node_counts[:, None], (group_size, rows_dev)).reshape(-1)
    live = (position < limits).astype(jnp.float32)[:, None]
    width = shard.shape[2]
    weights = lax.all_gather(shard, "node", axis=1, tiled=True)
    gate = jnp.dot(tokens, weights[0], preferred_element_type=jnp.float32)
    up = jnp.dot(tokens, weights[1], preferred_element_type=jnp.float32)
    sigmoid_gate = jax.nn.sigmoid(gate)
    activated = gate * sigmoid_gate
    hidden = (live * activated * up).astype(jnp.bfloat16)
    upstream = live * hidden_grad.astype(jnp.float32)
    gate_cot = (upstream * up * sigmoid_gate * (1.0 + gate * (1.0 - sigmoid_gate))).astype(
        jnp.bfloat16
    )
    up_cot = (upstream * activated).astype(jnp.bfloat16)
    cot_pair = jnp.concatenate([gate_cot, up_cot], axis=1)
    scale = 1.0 / jnp.sqrt(jnp.float32(rows_node * lax.axis_size("node")))
    contract = (((0,), (0,)), ((), ()))
    partial_grad = (
        lax.dot_general(tokens, cot_pair, contract, preferred_element_type=jnp.float32) * scale
    )
    share = lax.psum_scatter(partial_grad, "node", scatter_dimension=0, tiled=True)
    weight_grad = jnp.stack([share[:, :width], share[:, width:]])
    return (hidden, weight_grad)


def solution(mesh):
    return jax.shard_map(
        on_device,
        mesh=mesh,
        in_specs=(
            P("node", None),
            P("node", "local"),
            P(None, "node", "local"),
            P(("node", "local")),
        ),
        out_specs=(P("node", "local"), P(None, "node", "local")),
        check_vma=False,
    )
```

profile of v0, /device:TPU:1, one launch (start us, length us, event | category | flops | bytes accessed | tf_op | source)
XLA Modules:
  0.0 1122.0 jit_solution(2198829415349025462)
XLA Ops:
  7.2 0.0 copy-start.2
  7.2 0.0 all-gather.2.cloned.1.call-start
  7.2 1.4 convert_element_type.23
  8.6 0.0 all-gather.2.cloned.1.call-update
  8.6 0.0 reduce-scatter.4.cloned.1.call-start
  9.3 1.3 dynamic-slice
  10.6 0.8 dynamic-update-slice
  11.4 25.9 %all-reduce = s32[8]{0:T(128)S(1)} all-reduce(s32[8]{0:T(128)S(1)} %dynamic-update-slice), channel_id=1, replica_groups=mesh['node'=128,'local'=8] {'local'}, use_global_device_ids=true, to_apply=%add | all-reduce | flops 8 | bytes 64
  37.2 0.1 fusion.11
  37.3 207.5 %all-gather.2.cloned.1.call-done = bf16[2,4096,96]{2,1,0:T(8,128)(2,1)} async-done(((bf16[2,32,96]{2,1,0:T(8,128)(2,1)}), bf16[2,4096,96]{2,1,0:T(8,128)(2,1)}) %all-gather.2.cloned.1.call-update) | async-done | bytes 1572880 | tf_op jit(solution)/shard_map/all_gather | solution.py:17
  244.8 0.0 copy-start
  244.8 0.0 copy-start.1
  244.8 6.4 fusion.1
  251.2 0.0 copy-done.2
  251.3 0.0 copy-done
  251.3 0.2 copy-done.1
  251.5 3.5 multiply_convert_fusion.1
  255.0 1.8 fusion
  256.8 3.3 copy.9
  260.1 0.0 reduce-scatter.4.cloned.1.call-update
  260.1 853.1 %reduce-scatter.4.cloned.1.call-done = f32[32,192]{1,0:T(8,128)} async-done(((f32[4096,192]{1,0:T(8,128)}), f32[32,192]{1,0:T(8,128)}) %reduce-scatter.4.cloned.1.call-update) | async-done | bytes 24592
  1113.3 0.9 fusion.13
  1114.2 0.1 copy.11
  1114.3 0.1 copy.7
  1114.3 0.1 copy.12
  1114.4 0.1 copy.8
  1114.5 0.6 pad_maximum_fusion
  (1 shorter events, 0.0 us)
Async XLA Ops:
  7.2 244.1 %copy-start.2 = (bf16[1024,96]{0,1:T(8,128)(2,1)S(1)}, bf16[1024,96]{0,1:T(8,128)(2,1)}, u32[]{:S(2)}) copy-start(bf16[1024,96]{0,1:T(8,128)(2,1)} %param.5) | copy-start | bytes 589828
  7.2 237.6 %all-gather.2.cloned.1.call-start = ((), (), s32[]{:S(2)}) async-start(), calls=%async_computation.1 | async-start | bytes 2113536 | tf_op jit(solution)/shard_map/all_gather | solution.py:17
  8.6 1104.6 %reduce-scatter.4.cloned.1.call-start = ((), (), s32[]{:S(2)}) async-start(), calls=%async_computation.2 | async-start | bytes 4227072
  244.8 6.5 copy-start
  244.8 6.7 copy-start.1
Sparse Core Ops, SparseCore 0:
  11.3 233.4 all-gather.1
  260.3 852.9 reduce-scatter.3
where the time goes:
time: 1130 us; the launch traced here: 1120 us
  waiting for transfers between devices  1060 us (94%)
  blocking collectives  25.9 us (2%)
  between operations  14.7 us (1%)
  matrix products  11.8 us (1%)
    unnamed x3, waiting for transfers between devices  853 us
    all_gather x1, waiting for transfers between devices, on_device(): weights = lax.all_gather(shard, 'node', axis=1, tiled=True)  207 us
    unnamed x1, blocking collectives  25.9 us
  transfers between devices with their start and end apart: 2, of which 2 were waited for; matrix products, arithmetic and copies ran while one was open for 0% of the time, Pallas kernels for 0%

commit v1 on v0

v1 whole, which is shorter than its diff:
```python
import jax
import jax.numpy as jnp
from jax import lax
from jax.experimental import pallas as pl
from jax.experimental.pallas import tpu as pltpu
from jax.sharding import PartitionSpec as P

BF16 = jnp.bfloat16
F32 = jnp.float32
MESH = pl.DeviceIdType.MESH

NZ, NY = 8, 8
ROWS, WIDTH = 32, 96
PACKED = 48


def pack(block):
    tail = jnp.concatenate([block[..., :16, 128:192], block[..., 16:32, 128:192]], axis=-1)
    return jnp.concatenate([block[..., :128], tail], axis=-2)


def kernel(
    tok_hbm, hg_hbm, master_ref, counts_ref,
    hid_hbm, wg_ref,
    tok, tokT, hg, hgT, wbuf, w_y, acc, cotT, hidT, hid, cnt,
    part, xsend, xrecv, rsend, rrecv, own, zsend, zrecv,
    tok_sem, hg_sem, hid_sem,
    cnt_s, cnt_r, az_s, az_r, ay_s, ay_r, ac_s, ac_r,
    rc_s, rc_r, ry_s, ry_r, rz_s, rz_r,
):
    node, loc = lax.axis_index("node"), lax.axis_index("local")
    z, y, c = node // (2 * NY), (node // 2) % NY, node % 2
    rows = tok.shape[1]
    chunk = tok.shape[2]

    def at(z_, y_, c_):
        return ((z_ * NY + y_) * 2 + c_, loc)

    def ring(offset):
        return lax.rem(y + offset + 2 * NY, NY)

    right, left, twin = at(z, ring(1), c), at(z, ring(-1), c), at(z, y, 1 - c)
    z_peers = [at(lax.rem(z + i, NZ), y, c) for i in range(1, NZ)]
    l_peers = [(node, lax.rem(loc + i, 8)) for i in range(1, 8)]

    tok_copies = [
        pltpu.make_async_copy(tok_hbm.at[:, pl.ds(i * chunk, chunk)], tok.at[i], tok_sem.at[i])
        for i in range(NZ)
    ]
    hg_copy = pltpu.make_async_copy(hg_hbm, hg, hg_sem)
    barrier = pltpu.get_barrier_semaphore()
    peers = [right, left, twin] + z_peers + l_peers
    for peer in peers:
        pl.semaphore_signal(barrier, inc=1, device_id=peer, device_id_type=MESH)
    for copy in tok_copies:
        copy.start()
    hg_copy.start()
    both = jnp.concatenate([master_ref[0], master_ref[1]], axis=1)
    wbuf[c, y, z] = pack(both).astype(BF16)
    cnt[loc] = jnp.full((8, 128), counts_ref[0], jnp.int32)
    pl.semaphore_wait(barrier, len(peers))

    sends = []

    def remote(src, dst, s_sem, r_sem, device):
        return pltpu.make_async_remote_copy(
            src_ref=src, dst_ref=dst, send_sem=s_sem, recv_sem=r_sem,
            device_id=device, device_id_type=MESH,
        )

    def push(copy):
        copy.start()
        sends.append(copy)

    for i in range(1, NZ):
        push(remote(wbuf.at[c, y, z], wbuf.at[c, y, z], az_s.at[i], az_r.at[z], z_peers[i - 1]))
    for i in range(1, 8):
        push(remote(cnt.at[loc], cnt.at[loc], cnt_s.at[i], cnt_r.at[loc], l_peers[i - 1]))

    near = z // 4

    def half(k):
        return near if k == 0 else 1 - near

    def transpose(i):
        tok_copies[i].wait()
        tokT[i] = tok[i].T.reshape(NY, chunk // NY, rows)

    def ay(d, s, k):
        origin = ring(1 - s) if d == 0 else ring(s - 1)
        block = wbuf.at[c, origin, pl.ds(4 * half(k), 4)]
        return remote(block, block, ay_s.at[d, s - 1, k], ay_r.at[d, s - 1, k], right if d == 0 else left)

    def ac(offset, k, to=None):
        block = wbuf.at[c if to is None else 1 - c, ring(offset), pl.ds(4 * half(k), 4)]
        return remote(block, block, ac_s.at[offset % NY, k], ac_r.at[offset % NY, k], twin)

    def forward(offset):
        for k in range(2):
            ac(offset, k, to=0).wait_recv()
        o = ring(offset)
        for core in range(2):
            for j in range(NZ):
                r = j * 64 + core * ROWS
                got = wbuf[core, o, j]
                w_y[r : r + ROWS, :128] = got[:ROWS]
                w_y[r : r + 16, 128:192] = got[ROWS:, :64]
                w_y[r + 16 : r + 32, 128:192] = got[ROWS:, 64:]
        x = tokT[:, o].reshape(chunk, rows)
        d = lax.dot_general(w_y[...], x, (((0,), (0,)), ((), ())), preferred_element_type=F32)
        if offset == 0:
            acc[...] = d
        else:
            acc[...] += d

    for i in range(4):
        transpose(i)
    for k in range(2):
        for j in range(4):
            origin = 4 * half(k) + j

            @pl.when(origin != z)
            def _():
                block = wbuf.at[c, y, origin]
                remote(block, block, az_s.at[0], az_r.at[origin], twin).wait_recv()

        for d in range(2):
            push(ay(d, 1, k))
        push(ac(0, k))
        if k == 0:
            for i in range(4, 8):
                transpose(i)
    hg_copy.wait()
    hgT[...] = hg[...].T
    for s in range(2, 6):
        for k in range(2):
            for d in range(2):
                if s - 1 == 4 and d != k:
                    continue
                ay(d, s - 1, k).wait_recv()
                if s <= 3 or (s == 4 and d == k):
                    push(ay(d, s, k))
                push(ac(1 - s if d == 0 else s - 1, k) if s < 5 else ac(4, k))
        if s == 2:
            forward(0)
        elif s > 2:
            forward(s - 2)
            forward(2 - s)
    for i in range(1, 8):
        slot = cnt.at[lax.rem(loc + i, 8)]
        remote(slot, slot, cnt_s.at[0], cnt_r.at[lax.rem(loc + i, 8)], twin).wait_recv()
    forward(4)

    for j in range(8):
        lanes = slice(j * 128, (j + 1) * 128)
        live = (lax.broadcasted_iota(jnp.int32, (8, 128), 1) < cnt[j]).astype(F32)[:1]
        gate, up = acc[:WIDTH, lanes], acc[WIDTH:, lanes]
        sig = jax.nn.sigmoid(gate)
        activated = gate * sig
        hidT[:, lanes] = (live * activated * up).astype(BF16)
        upstream = live * hgT[:, lanes].astype(F32)
        cotT[:WIDTH, lanes] = (upstream * up * sig * (1.0 + gate * (1.0 - sig))).astype(BF16)
        cotT[WIDTH:, lanes] = (upstream * activated).astype(BF16)

    def rc(offset):
        i = offset % NY
        return remote(xsend.at[i], xrecv.at[i], rc_s.at[i], rc_r.at[i], twin)

    def backward(offset):
        i = offset % NY
        x = tokT[:, ring(offset)].reshape(chunk, rows)
        g = lax.dot_general(x, cotT[...], (((1,), (1,)), ((), ())), preferred_element_type=F32)
        part[i] = g.reshape(NZ, 2, ROWS, 2 * WIDTH)
        xsend[i] = pack(part[i, :, 1 - c]).astype(BF16)
        push(rc(offset))

    def chip_sum(offset):
        i = offset % NY
        rc(offset).wait_recv()
        own[i] = pack(part[i, :, c]) + xrecv[i].astype(F32)

    def ry(d, s, k):
        h = pl.ds(4 * half(k), 4)
        return remote(
            rsend.at[d, s - 1, h], rrecv.at[d, s - 1, h],
            ry_s.at[d, s - 1, k], ry_r.at[d, s - 1, k], right if d == 0 else left,
        )

    def ry_send(s):
        for k in range(2):
            for d in range(2):
                if s == 1 and d != k:
                    continue
                h = pl.ds(4 * half(k), 4)
                mine = own[(5 - s if d == 0 else s - 5) % NY, h]
                if s > 2 or (s == 2 and d == k):
                    ry(d, s - 1, k).wait_recv()
                    mine = mine + rrecv[d, s - 2, h].astype(F32)
                rsend[d, s - 1, h] = mine.astype(BF16)
                push(ry(d, s, k))

    backward(4)
    backward(3)
    chip_sum(4)
    ry_send(1)
    backward(-3)
    chip_sum(3)
    backward(2)
    chip_sum(-3)
    ry_send(2)
    backward(-2)
    chip_sum(2)
    backward(1)
    chip_sum(-2)
    ry_send(3)
    backward(-1)
    chip_sum(1)
    backward(0)
    chip_sum(-1)
    ry_send(4)
    chip_sum(0)
    hid[...] = hidT[...].T
    hid_copy = pltpu.make_async_copy(hid, hid_hbm, hid_sem)
    hid_copy.start()
    total = own[0]
    for d in range(2):
        for k in range(2):
            ry(d, 4, k).wait_recv()
        total = total + rrecv[d, 3].astype(F32)
    own[0] = total
    zsend[...] = total.astype(BF16)
    for i in range(1, NZ):
        to = lax.rem(z + i, NZ)
        push(remote(zsend.at[to], zrecv.at[i], rz_s.at[i], rz_r.at[i], z_peers[i - 1]))
    grad = own[0, z]
    for i in range(1, NZ):
        remote(zsend.at[0], zrecv.at[i], rz_s.at[i], rz_r.at[i], twin).wait_recv()
        grad = grad + zrecv[i].astype(F32)
    grad = grad * (1.0 / (rows * NZ * NY * 2) ** 0.5)
    tail = jnp.concatenate([grad[ROWS:, :64], grad[ROWS:, 64:]], axis=0)
    wg_ref[0] = grad[:ROWS, :WIDTH]
    wg_ref[1] = jnp.concatenate([grad[:ROWS, WIDTH:], tail], axis=1)
    for copy in sends:
        copy.wait_send()
    hid_copy.wait()


def on_device(tokens, hidden_grad, master, counts):
    rows, depth = tokens.shape
    chunk = depth // NZ
    dma = pltpu.SemaphoreType.DMA
    vmem = pltpu.VMEM
    return pl.pallas_call(
        kernel,
        out_shape=(
            jax.ShapeDtypeStruct(hidden_grad.shape, BF16),
            jax.ShapeDtypeStruct(master.shape, F32),
        ),
        in_specs=[
            pl.BlockSpec(memory_space=pl.ANY),
            pl.BlockSpec(memory_space=pl.ANY),
            pl.BlockSpec(memory_space=vmem),
            pl.BlockSpec(memory_space=pltpu.SMEM),
        ],
        out_specs=(pl.BlockSpec(memory_space=pl.ANY), pl.BlockSpec(memory_space=vmem)),
        scratch_shapes=[
            vmem((NZ, rows, chunk), BF16),
            vmem((NZ, NY, chunk // NY, rows), BF16),
            vmem((rows, WIDTH), BF16),
            vmem((WIDTH, rows), BF16),
            vmem((2, NY, NZ, PACKED, 128), BF16),
            vmem((chunk, 2 * WIDTH), BF16),
            vmem((2 * WIDTH, rows), F32),
            vmem((2 * WIDTH, rows), BF16),
            vmem((WIDTH, rows), BF16),
            vmem((rows, WIDTH), BF16),
            vmem((8, 8, 128), jnp.int32),
            vmem((NY, NZ, 2, ROWS, 2 * WIDTH), F32),
            vmem((NY, NZ, PACKED, 128), BF16),
            vmem((NY, NZ, PACKED, 128), BF16),
            vmem((2, 4, NZ, PACKED, 128), BF16),
            vmem((2, 4, NZ, PACKED, 128), BF16),
            vmem((NY, NZ, PACKED, 128), F32),
            vmem((NZ, PACKED, 128), BF16),
            vmem((NZ, PACKED, 128), BF16),
            dma((NZ,)), dma, dma,
            dma((8,)), dma((8,)), dma((NZ,)), dma((NZ,)),
            dma((2, 4, 2)), dma((2, 4, 2)), dma((NY, 2)), dma((NY, 2)),
            dma((NY,)), dma((NY,)), dma((2, 4, 2)), dma((2, 4, 2)), dma((NZ,)), dma((NZ,)),
        ],
        compiler_params=pltpu.CompilerParams(
            collective_id=1, has_side_effects=True, vmem_limit_bytes=56 * 2**20
        ),
    )(tokens, hidden_grad, master, counts)


def solution(mesh):
    return jax.shard_map(
        on_device,
        mesh=mesh,
        in_specs=(
            P("node", None),
            P("node", "local"),
            P(None, "node", "local"),
            P(("node", "local")),
        ),
        out_specs=(P("node", "local"), P(None, "node", "local")),
        check_vma=False,
    )
```

time: 1130 us -> 80.9 us (0.07)
  waiting for transfers between devices: 1060 us -> 0 us
  Pallas kernels: 0 us -> 74.4 us
  blocking collectives: 25.9 us -> 0 us
  between operations: 14.7 us -> 1.29 us
  matrix products: 11.8 us -> 0 us
    unnamed x3 -> x0, waiting for transfers between devices: 853 us -> none
    all_gather x1 -> x0, waiting for transfers between devices: 207 us -> none  [on_device(): weights = lax.all_gather(shard, 'node', axis=1, tiled=True)]
    pallas_call x0 -> x1, Pallas kernels: none -> 74.4 us  [on_device(): pl.pallas_call(kernel, out_shape=(jax.ShapeDtypeStruct(hidden_grad.shape,...]
    unnamed x1 -> x0, blocking collectives: 25.9 us -> none
    dot_general x3 -> x0, matrix products: 11.8 us -> none  [the longest x1 6.44 us: on_device(): up = jnp.dot(tokens, weights[1], preferred_element_type=jnp.float32)]
  transfers between devices with their start and end apart: 2 -> 0, of which waited for: 2 -> 0; matrix products, arithmetic and copies ran while one was open for 0% -> 0% of each run, Pallas kernels for 0% -> 0%
where the time goes in v1:
time: 80.9 us; the launch traced here: 80.5 us
  Pallas kernels  74.4 us (92%)
  local copies, waits for them, and re-layouts  4.89 us (6%)
  between operations  1.29 us (2%)
    pallas_call x1, Pallas kernels, on_device(): pl.pallas_call(kernel, out_shape=(jax.ShapeDtypeStruct(hidden_grad.shape,...  74.4 us
    unnamed x2, local copies, waits for them, and re-layouts  3.13 us
    pallas_call x1, local copies, waits for them, and re-layouts, on_device(): pl.pallas_call(kernel, out_shape=(jax.ShapeDtypeStruct(hidden_grad.shape,...  1.76 us

profile of v1, /device:TPU:1, one launch (start us, length us, event | category | flops | bytes accessed | tf_op | source)
XLA Modules:
  0.0 80.5 jit_solution(8466186048874294226)
XLA Ops:
  1.3 1.8 %copy.6.hg_hbm = bf16[1024,96]{1,0:T(8,128)(2,1)} copy(bf16[1024,96]{0,1:T(8,128)(2,1)} %param.5) | data formatting | bytes 393216 | tf_op args[1]
  3.0 74.4 %shard_map.59 = (bf16[1024,96]{1,0:T(8,128)(2,1)}, f32[2,32,96]{2,1,0:T(8,128)}) custom-call(bf16[1024,4096]{1,0:T(8,128)(2,1)} %tok_hbm.1, bf16[1024,96]{1,0:T(8,128)(2,1)} %copy.6.hg_hbm, f32[2,32,96]{2,1,0:T(8,128)} %master_ref.1, s32[1]{0:T(128)S(6)} %copy.9.counts_ref), custom_call_target="tpu_custom_call" | custom-call | tf_op jit(solution)/shard_map/pallas_call | solution.py:253
  77.4 1.8 %copy.7 = bf16[1024,96]{0,1:T(8,128)(2,1)} copy(bf16[1024,96]{1,0:T(8,128)(2,1)} %get-tuple-element.2) | data formatting | bytes 393216 | tf_op jit(solution)/shard_map/pallas_call | solution.py:253
  79.2 1.4 %copy.10 = f32[2,32,96]{2,1,0:T(8,128)} copy(f32[2,32,96]{2,1,0:T(8,128)} %get-tuple-element.7) | data formatting | bytes 49152

commit v2 on v1

v2 whole, which is shorter than its diff:
```python
import jax
import jax.numpy as jnp
from jax import lax
from jax.experimental import pallas as pl
from jax.experimental.pallas import tpu as pltpu
from jax.sharding import PartitionSpec as P

BF16 = jnp.bfloat16
F32 = jnp.float32
MESH = pl.DeviceIdType.MESH

NZ, NY = 8, 8
ROWS, WIDTH = 32, 96
PACKED = 48


def pack(block):
    tail = jnp.concatenate([block[..., :16, 128:192], block[..., 16:32, 128:192]], axis=-1)
    return jnp.concatenate([block[..., :128], tail], axis=-2)


def kernel(
    tok_hbm, hgT_hbm, master_ref, counts_ref,
    hidT_hbm, wg_ref,
    tok, tokT, hgT, wbuf, w_y, acc, cotT, hidT, cnt,
    part, xsend, xrecv, rsend, rrecv, own, zsend, zrecv,
    tok_sem, hg_sem, hid_sem,
    cx_s, cx_r, ch_s, ch_r, az_u, az_d, az_r, ay_s, ay_r, ac_s, ac_r,
    rc_s, rc_r, ry_s, ry_r, rz_s, rz_r,
):
    node, loc = lax.axis_index("node"), lax.axis_index("local")
    z, y, c = node // (2 * NY), (node // 2) % NY, node % 2
    zh, x = loc // 4, loc % 4
    rows = tok.shape[1]
    chunk = tok.shape[2]

    def at(z_, y_, c_):
        return ((z_ * NY + y_) * 2 + c_, loc)

    def ring(offset):
        return lax.rem(y + offset + 2 * NY, NY)

    right, left, twin = at(z, ring(1), c), at(z, ring(-1), c), at(z, y, 1 - c)
    x_peers = [(node, zh * 4 + lax.rem(x + i, 4)) for i in range(1, 4)]
    partner = (node, (1 - zh) * 4 + x)

    tok_copies = [
        pltpu.make_async_copy(tok_hbm.at[:, pl.ds(i * chunk, chunk)], tok.at[i], tok_sem.at[i])
        for i in range(NZ)
    ]
    hg_copy = pltpu.make_async_copy(hgT_hbm, hgT, hg_sem)
    hid_copy = pltpu.make_async_copy(hidT, hidT_hbm, hid_sem)

    barrier = pltpu.get_barrier_semaphore()

    def greet(peer):
        pl.semaphore_signal(barrier, inc=1, device_id=peer, device_id_type=MESH)

    for i in range(1, NZ):

        @pl.when(z + i < NZ)
        def _():
            greet(at(z + i, y, c))

    @pl.when(z > 0)
    def _():
        greet(at(z - 1, y, c))

    @pl.when(zh == 0)
    def _():
        greet(partner)

    for peer in [right, left, twin] + x_peers:
        greet(peer)
    for copy in tok_copies:
        copy.start()
    hg_copy.start()
    both = jnp.concatenate([master_ref[0], master_ref[1]], axis=1)
    wbuf[c, y, z] = pack(both).astype(BF16)
    cnt[loc] = jnp.full((8, 128), counts_ref[0], jnp.int32)
    pl.semaphore_wait(barrier, 6 + z + zh + jnp.where(z < NZ - 1, 1, 0))

    sends = []

    def remote(src, dst, s_sem, r_sem, device):
        return pltpu.make_async_remote_copy(
            src_ref=src, dst_ref=dst, send_sem=s_sem, recv_sem=r_sem,
            device_id=device, device_id_type=MESH,
        )

    def push(copy):
        copy.start()
        sends.append(copy)

    def transpose(i):
        tok_copies[i].wait()
        tokT[i] = tok[i].T.reshape(NY, chunk // NY, rows)

    pz, ph = z // 2, z // 4
    pairs = [pz, ph * 4 + 1 - pz, 2 - ph, 3 - 3 * ph]

    def pair(k):
        return pl.ds(2 * pairs[k], 2)

    def az_down(i):
        block = wbuf.at[c, y, z]
        return remote(block, block, az_d.at[i], az_r.at[z], at(z - i, y, c))

    def az_up(i):
        block = wbuf.at[c, y, z - i]
        return remote(block, block, az_u.at[i], az_r.at[z - i], at(z + 1, y, c))

    def az_wait(origin):
        block = wbuf.at[c, y, origin]
        remote(block, block, az_u.at[0], az_r.at[origin], twin).wait_recv()

    def relay(i):
        @pl.when(z >= i)
        def _():
            az_wait(z - i)

            @pl.when(z < NZ - 1)
            def _():
                az_up(i).start()

    @pl.when(z < NZ - 1)
    def _():
        az_up(0).start()

    for i in range(NZ - 1, 0, -1):

        @pl.when(z >= i)
        def _():
            az_down(i).start()

    for i in range(3):
        push(remote(cnt.at[loc], cnt.at[loc], cx_s.at[i], cx_r.at[2 - i], x_peers[i]))

    def ay(d, s, k):
        origin = ring(1 - s) if d == 0 else ring(s - 1)
        block = wbuf.at[c, origin, pair(k)]
        return remote(block, block, ay_s.at[d, s - 1, k], ay_r.at[d, s - 1, k], right if d == 0 else left)

    def ac(offset, k, core):
        block = wbuf.at[core, ring(offset), pair(k)]
        return remote(block, block, ac_s.at[offset % NY, k], ac_r.at[offset % NY, k], twin)

    def forward(offset):
        for k in range(4):
            ac(offset, k, 1 - c).wait_recv()
        o = ring(offset)
        for core in range(2):
            for j in range(NZ):
                r = j * 64 + core * ROWS
                got = wbuf[core, o, j]
                w_y[r : r + ROWS, :128] = got[:ROWS]
                w_y[r : r + 16, 128:192] = got[ROWS:, :64]
                w_y[r + 16 : r + 32, 128:192] = got[ROWS:, 64:]
        v = tokT[:, o].reshape(chunk, rows)
        d = lax.dot_general(w_y[...], v, (((0,), (0,)), ((), ())), preferred_element_type=F32)
        if offset == 0:
            acc[...] = d
        else:
            acc[...] += d

    def gather(k, s):
        if s == 0:
            for i in range(2):
                origin = 2 * pairs[k] + i

                @pl.when(origin > z)
                def _():
                    az_wait(origin)

            for d in range(2):
                push(ay(d, 1, k))
            push(ac(0, k, c))
            return
        for d in range(2):
            if s == 4 and d != k % 2:
                continue
            ay(d, s, k).wait_recv()
            if s < 3 or (s == 3 and d == k % 2):
                push(ay(d, s + 1, k))
            push(ac(4 if s == 4 else (-s if d == 0 else s), k, c))

    own_row = cnt.at[pl.ds(zh * 4, 4)]
    other_row = cnt.at[pl.ds((1 - zh) * 4, 4)]
    row_out = remote(own_row, own_row, ch_s, ch_r, partner)
    row_in = remote(other_row, other_row, ch_s, ch_r, partner)

    for t in range(8):
        if t < 4:
            transpose(2 * t)
            transpose(2 * t + 1)
            for i in range(2 * t, 2 * t + 2):
                if i > 0:
                    relay(i)
        elif t == 4:
            forward(0)
        else:
            forward(t - 4)
            forward(4 - t)
        for k in range(4):
            if 0 <= t - k <= 4:
                gather(k, t - k)
        if t == 1:
            for i in range(3):
                slot = cnt.at[zh * 4 + lax.rem(x + 3 - i, 4)]
                remote(slot, slot, cx_s.at[i], cx_r.at[2 - i], twin).wait_recv()

            @pl.when(zh == 1)
            def _():
                row_out.start()

    row_in.wait_recv()

    @pl.when(zh == 0)
    def _():
        row_out.start()

    forward(4)

    for j in range(8):
        lanes = slice(j * 128, (j + 1) * 128)
        live = (lax.broadcasted_iota(jnp.int32, (8, 128), 1) < cnt[j]).astype(F32)[:1]
        gate, up = acc[:WIDTH, lanes], acc[WIDTH:, lanes]
        if j == 0:
            hg_copy.wait()
        sig = jax.nn.sigmoid(gate)
        activated = gate * sig
        hidT[:, lanes] = (live * activated * up).astype(BF16)
        upstream = live * hgT[:, lanes].astype(F32)
        cotT[:WIDTH, lanes] = (upstream * up * sig * (1.0 + gate * (1.0 - sig))).astype(BF16)
        cotT[WIDTH:, lanes] = (upstream * activated).astype(BF16)
    hid_copy.start()

    def rc(offset):
        i = offset % NY
        return remote(xsend.at[i], xrecv.at[i], rc_s.at[i], rc_r.at[i], twin)

    def backward(offset):
        i = offset % NY
        v = tokT[:, ring(offset)].reshape(chunk, rows)
        g = lax.dot_general(v, cotT[...], (((1,), (1,)), ((), ())), preferred_element_type=F32)
        part[i] = g.reshape(NZ, 2, ROWS, 2 * WIDTH)
        xsend[i] = pack(part[i, :, 1 - c]).astype(BF16)
        push(rc(offset))

    def chip_sum(offset):
        i = offset % NY
        rc(offset).wait_recv()
        own[i] = pack(part[i, :, c]) + xrecv[i].astype(F32)

    def ry(d, s, k):
        return remote(
            rsend.at[d, s - 1, pair(k)], rrecv.at[d, s - 1, pair(k)],
            ry_s.at[d, s - 1, k], ry_r.at[d, s - 1, k], right if d == 0 else left,
        )

    def ry_send(s):
        for k in range(3, -1, -1):
            for d in range(2):
                if s == 1 and d != k % 2:
                    continue
                mine = own[(5 - s if d == 0 else s - 5) % NY, pair(k)]
                if s > 2 or (s == 2 and d == k % 2):
                    ry(d, s - 1, k).wait_recv()
                    mine = mine + rrecv[d, s - 2, pair(k)].astype(F32)
                rsend[d, s - 1, pair(k)] = mine.astype(BF16)
                push(ry(d, s, k))

    backward(4)
    backward(3)
    chip_sum(4)
    ry_send(1)
    backward(-3)
    chip_sum(3)
    backward(2)
    chip_sum(-3)
    ry_send(2)
    backward(-2)
    chip_sum(2)
    backward(1)
    chip_sum(-2)
    ry_send(3)
    backward(-1)
    chip_sum(1)
    backward(0)
    chip_sum(-1)
    ry_send(4)
    chip_sum(0)
    zrecv[z] = jnp.zeros(zrecv.shape[1:], BF16)

    def rz(to):
        return remote(zsend.at[to], zrecv.at[z], rz_s.at[to], rz_r.at[z], at(to, y, c))

    for k in range(3, -1, -1):
        total = own[0, pair(k)]
        for d in range(2):
            ry(d, 4, k).wait_recv()
            total = total + rrecv[d, 3, pair(k)].astype(F32)
        own[0, pair(k)] = total
        zsend[pair(k)] = total.astype(BF16)
        for i in range(2):
            to = 2 * pairs[k] + i

            @pl.when(to != z)
            def _():
                rz(to).start()

    for j in range(NZ):

        @pl.when(z != j)
        def _():
            remote(zsend.at[j], zrecv.at[j], rz_s.at[j], rz_r.at[j], twin).wait_recv()

    grad = own[0, z]
    for j in range(NZ):
        grad = grad + zrecv[j].astype(F32)
    grad = grad * (1.0 / (rows * NZ * NY * 2) ** 0.5)
    tail = jnp.concatenate([grad[ROWS:, :64], grad[ROWS:, 64:]], axis=0)
    wg_ref[0] = grad[:ROWS, :WIDTH]
    wg_ref[1] = jnp.concatenate([grad[:ROWS, WIDTH:], tail], axis=1)
    for copy in sends:
        copy.wait_send()
    row_out.wait_send()
    for i in range(NZ):

        @pl.when(jnp.logical_and(z >= i, z < NZ - 1))
        def _():
            az_up(i).wait_send()

        if i > 0:

            @pl.when(z >= i)
            def _():
                az_down(i).wait_send()

        @pl.when(z != i)
        def _():
            rz(i).wait_send()

    hid_copy.wait()


def on_device(tokens, hidden_grad, master, counts):
    rows, depth = tokens.shape
    chunk = depth // NZ
    dma = pltpu.SemaphoreType.DMA
    vmem = pltpu.VMEM
    hidden, weight_grad = pl.pallas_call(
        kernel,
        out_shape=(
            jax.ShapeDtypeStruct((WIDTH, rows), BF16),
            jax.ShapeDtypeStruct(master.shape, F32),
        ),
        in_specs=[
            pl.BlockSpec(memory_space=pl.ANY),
            pl.BlockSpec(memory_space=pl.ANY),
            pl.BlockSpec(memory_space=vmem),
            pl.BlockSpec(memory_space=pltpu.SMEM),
        ],
        out_specs=(pl.BlockSpec(memory_space=pl.ANY), pl.BlockSpec(memory_space=vmem)),
        scratch_shapes=[
            vmem((NZ, rows, chunk), BF16),
            vmem((NZ, NY, chunk // NY, rows), BF16),
            vmem((WIDTH, rows), BF16),
            vmem((2, NY, NZ, PACKED, 128), BF16),
            vmem((chunk, 2 * WIDTH), BF16),
            vmem((2 * WIDTH, rows), F32),
            vmem((2 * WIDTH, rows), BF16),
            vmem((WIDTH, rows), BF16),
            vmem((8, 8, 128), jnp.int32),
            vmem((NY, NZ, 2, ROWS, 2 * WIDTH), F32),
            vmem((NY, NZ, PACKED, 128), BF16),
            vmem((NY, NZ, PACKED, 128), BF16),
            vmem((2, 4, NZ, PACKED, 128), BF16),
            vmem((2, 4, NZ, PACKED, 128), BF16),
            vmem((NY, NZ, PACKED, 128), F32),
            vmem((NZ, PACKED, 128), BF16),
            vmem((NZ, PACKED, 128), BF16),
            dma((NZ,)), dma, dma,
            dma((3,)), dma((3,)), dma, dma, dma((NZ,)), dma((NZ,)), dma((NZ,)),
            dma((2, 4, 4)), dma((2, 4, 4)), dma((NY, 4)), dma((NY, 4)),
            dma((NY,)), dma((NY,)), dma((2, 4, 4)), dma((2, 4, 4)), dma((NZ,)), dma((NZ,)),
        ],
        compiler_params=pltpu.CompilerParams(
            collective_id=1, has_side_effects=True, vmem_limit_bytes=56 * 2**20
        ),
    )(tokens, hidden_grad.T, master, counts)
    return hidden.T, weight_grad


def solution(mesh):
    return jax.shard_map(
        on_device,
        mesh=mesh,
        in_specs=(
            P("node", None),
            P("node", "local"),
            P(None, "node", "local"),
            P(("node", "local")),
        ),
        out_specs=(P("node", "local"), P(None, "node", "local")),
        check_vma=False,
    )
```

time: 80.9 us -> 79.4 us (0.981)
  local copies, waits for them, and re-layouts: 4.89 us -> 2.99 us
    pallas_call x1 -> x0, local copies, waits for them, and re-layouts: 1.76 us -> none  [on_device(): pl.pallas_call(kernel, out_shape=(jax.ShapeDtypeStruct(hidden_grad.shape,...]
where the time goes in v2:
time: 79.4 us; the launch traced here: 79.1 us
  Pallas kernels  74.8 us (94%)
  local copies, waits for them, and re-layouts  2.99 us (4%)
  between operations  1.29 us (2%)
    pallas_call x1, Pallas kernels, on_device(): pl.pallas_call(kernel, out_shape=(jax.ShapeDtypeStruct((WIDTH, rows), BF1...  74.8 us
    unnamed x2, local copies, waits for them, and re-layouts  2.99 us

profile of v2, /device:TPU:1, one launch (start us, length us, event | category | flops | bytes accessed | tf_op | source)
XLA Modules:
  0.0 79.1 jit_solution(11621125670901390550)
XLA Ops:
  1.3 74.8 %shard_map.59 = (bf16[96,1024]{1,0:T(8,128)(2,1)}, f32[2,32,96]{2,1,0:T(8,128)}) custom-call(bf16[1024,4096]{1,0:T(8,128)(2,1)} %tok_hbm.1, bf16[96,1024]{1,0:T(8,128)(2,1)} %bitcast.3, f32[2,32,96]{2,1,0:T(8,128)} %master_ref.1, s32[1]{0:T(128)S(6)} %copy.8.counts_ref), custom_call_target="tpu_custom_call" | custom-call | tf_op jit(solution)/shard_map/pallas_call | solution.py:352
  76.1 1.6 %copy.9 = bf16[1024,96]{0,1:T(8,128)(2,1)} copy(bf16[1024,96]{0,1:T(8,128)(2,1)} %bitcast.2) | data formatting | bytes 393216
  77.7 1.4 %copy.10 = f32[2,32,96]{2,1,0:T(8,128)} copy(f32[2,32,96]{2,1,0:T(8,128)} %get-tuple-element.9) | data formatting | bytes 49152

commit v3 on v2

--- a/solution.py
+++ b/solution.py
@@ -20,11 +20,11 @@
 
 
 def kernel(
-    tok_hbm, hgT_hbm, master_ref, counts_ref,
+    tok_hbm, hgT_hbm, master_hbm, counts_hbm,
     hidT_hbm, wg_ref,
-    tok, tokT, hgT, wbuf, w_y, acc, cotT, hidT, cnt,
+    master_ref, counts_ref, tok, tokT, hgT, wbuf, w_y, acc, cotT, hidT, cnt,
     part, xsend, xrecv, rsend, rrecv, own, zsend, zrecv,
-    tok_sem, hg_sem, hid_sem,
+    tok_sem, hg_sem, hid_sem, small_sem,
     cx_s, cx_r, ch_s, ch_r, az_u, az_d, az_r, ay_s, ay_r, ac_s, ac_r,
     rc_s, rc_r, ry_s, ry_r, rz_s, rz_r,
 ):
@@ -51,6 +51,15 @@
     hg_copy = pltpu.make_async_copy(hgT_hbm, hgT, hg_sem)
     hid_copy = pltpu.make_async_copy(hidT, hidT_hbm, hid_sem)
 
+    small = [
+        pltpu.make_async_copy(master_hbm, master_ref, small_sem.at[0]),
+        pltpu.make_async_copy(counts_hbm, counts_ref, small_sem.at[1]),
+    ]
+    for copy in small:
+        copy.start()
+
+    gate_z = NZ // 2 - 1
+    low = z % 4
     barrier = pltpu.get_barrier_semaphore()
 
     def greet(peer):
@@ -62,9 +71,15 @@
         def _():
             greet(at(z + i, y, c))
 
-    @pl.when(z > 0)
+    for i in range(1, 4):
+
+        @pl.when(low >= i)
+        def _():
+            greet(at(z - i, y, c))
+
+    @pl.when(z > gate_z)
     def _():
-        greet(at(z - 1, y, c))
+        greet(at(gate_z, y, c))
 
     @pl.when(zh == 0)
     def _():
@@ -72,13 +87,12 @@
 
     for peer in [right, left, twin] + x_peers:
         greet(peer)
-    for copy in tok_copies:
-        copy.start()
-    hg_copy.start()
+    for copy in small:
+        copy.wait()
     both = jnp.concatenate([master_ref[0], master_ref[1]], axis=1)
     wbuf[c, y, z] = pack(both).astype(BF16)
     cnt[loc] = jnp.full((8, 128), counts_ref[0], jnp.int32)
-    pl.semaphore_wait(barrier, 6 + z + zh + jnp.where(z < NZ - 1, 1, 0))
+    pl.semaphore_wait(barrier, 9 - low + z + zh + jnp.where(z == gate_z, 4, 0))
 
     sends = []
 
@@ -106,26 +120,29 @@
         block = wbuf.at[c, y, z]
         return remote(block, block, az_d.at[i], az_r.at[z], at(z - i, y, c))
 
-    def az_up(i):
-        block = wbuf.at[c, y, z - i]
-        return remote(block, block, az_u.at[i], az_r.at[z - i], at(z + 1, y, c))
+    def az_up(f, i):
+        block = wbuf.at[c, y, z - f]
+        return remote(block, block, az_u.at[f, i], az_r.at[z - f], at(z + i, y, c))
 
     def az_wait(origin):
         block = wbuf.at[c, y, origin]
-        remote(block, block, az_u.at[0], az_r.at[origin], twin).wait_recv()
-
-    def relay(i):
-        @pl.when(z >= i)
-        def _():
-            az_wait(z - i)
-
-            @pl.when(z < NZ - 1)
-            def _():
-                az_up(i).start()
-
-    @pl.when(z < NZ - 1)
-    def _():
-        az_up(0).start()
+        remote(block, block, az_d.at[0], az_r.at[origin], twin).wait_recv()
+
+    def up_has(i):
+        return jnp.logical_or(low + i < 4, z == gate_z)
+
+    def pass_up(f):
+        @pl.when(z == gate_z)
+        def _():
+            az_wait(z - f)
+            for i in range(4, 0, -1):
+                az_up(f, i).start()
+
+    for i in range(4, 0, -1):
+
+        @pl.when(up_has(i))
+        def _():
+            az_up(0, i).start()
 
     for i in range(NZ - 1, 0, -1):
 
@@ -135,6 +152,9 @@
 
     for i in range(3):
         push(remote(cnt.at[loc], cnt.at[loc], cx_s.at[i], cx_r.at[2 - i], x_peers[i]))
+    for copy in tok_copies:
+        copy.start()
+    hg_copy.start()
 
     def ay(d, s, k):
         origin = ring(1 - s) if d == 0 else ring(s - 1)
@@ -168,7 +188,7 @@
             for i in range(2):
                 origin = 2 * pairs[k] + i
 
-                @pl.when(origin > z)
+                @pl.when(jnp.logical_and(origin != z, jnp.logical_or(z != gate_z, origin > z)))
                 def _():
                     az_wait(origin)
 
@@ -190,12 +210,12 @@
     row_in = remote(other_row, other_row, ch_s, ch_r, partner)
 
     for t in range(8):
-        if t < 4:
-            transpose(2 * t)
-            transpose(2 * t + 1)
-            for i in range(2 * t, 2 * t + 2):
-                if i > 0:
-                    relay(i)
+        if t == 0:
+            pass_up(1)
+        elif t == 1:
+            pass_up(3)
+        elif t < 4:
+            pass
         elif t == 4:
             forward(0)
         else:
@@ -204,6 +224,10 @@
         for k in range(4):
             if 0 <= t - k <= 4:
                 gather(k, t - k)
+        if t == 0:
+            pass_up(2)
+        for i in ([0], [1, 2], [3, 4], [5, 6, 7], [], [], [], [])[t]:
+            transpose(i)
         if t == 1:
             for i in range(3):
                 slot = cnt.at[zh * 4 + lax.rem(x + 3 - i, 4)]
@@ -325,12 +349,18 @@
     for copy in sends:
         copy.wait_send()
     row_out.wait_send()
+    for i in range(1, 5):
+
+        @pl.when(up_has(i))
+        def _():
+            az_up(0, i).wait_send()
+
+        @pl.when(z == gate_z)
+        def _():
+            for f in range(1, 4):
+                az_up(f, i).wait_send()
+
     for i in range(NZ):
-
-        @pl.when(jnp.logical_and(z >= i, z < NZ - 1))
-        def _():
-            az_up(i).wait_send()
-
         if i > 0:
 
             @pl.when(z >= i)
@@ -342,6 +372,11 @@
             rz(i).wait_send()
 
     hid_copy.wait()
+
+
+def hand_out(hidden_in, grad_in, hidden_out, grad_out):
+    hidden_out[...] = hidden_in[...]
+    grad_out[...] = grad_in[...]
 
 
 def on_device(tokens, hidden_grad, master, counts):
@@ -358,11 +393,13 @@
         in_specs=[
             pl.BlockSpec(memory_space=pl.ANY),
             pl.BlockSpec(memory_space=pl.ANY),
-            pl.BlockSpec(memory_space=vmem),
-            pl.BlockSpec(memory_space=pltpu.SMEM),
+            pl.BlockSpec(memory_space=pltpu.HBM),
+            pl.BlockSpec(memory_space=pltpu.HBM),
         ],
         out_specs=(pl.BlockSpec(memory_space=pl.ANY), pl.BlockSpec(memory_space=vmem)),
         scratch_shapes=[
+            vmem(master.shape, F32),
+            pltpu.SMEM(counts.shape, jnp.int32),
             vmem((NZ, rows, chunk), BF16),
             vmem((NZ, NY, chunk // NY, rows), BF16),
             vmem((WIDTH, rows), BF16),
@@ -380,8 +417,8 @@
             vmem((NY, NZ, PACKED, 128), F32),
             vmem((NZ, PACKED, 128), BF16),
             vmem((NZ, PACKED, 128), BF16),
-            dma((NZ,)), dma, dma,
-            dma((3,)), dma((3,)), dma, dma, dma((NZ,)), dma((NZ,)), dma((NZ,)),
+            dma((NZ,)), dma, dma, dma((2,)),
+            dma((3,)), dma((3,)), dma, dma, dma((4, 5)), dma((NZ,)), dma((NZ,)),
             dma((2, 4, 4)), dma((2, 4, 4)), dma((NY, 4)), dma((NY, 4)),
             dma((NY,)), dma((NY,)), dma((2, 4, 4)), dma((2, 4, 4)), dma((NZ,)), dma((NZ,)),
         ],
@@ -389,6 +426,15 @@
             collective_id=1, has_side_effects=True, vmem_limit_bytes=56 * 2**20
         ),
     )(tokens, hidden_grad.T, master, counts)
+    hidden, weight_grad = pl.pallas_call(
+        hand_out,
+        out_shape=(
+            jax.ShapeDtypeStruct(hidden.shape, BF16),
+            jax.ShapeDtypeStruct(master.shape, F32),
+        ),
+        in_specs=[pl.BlockSpec(memory_space=vmem)] * 2,
+        out_specs=(pl.BlockSpec(memory_space=vmem),) * 2,
+    )(hidden, weight_grad)
     return hidden.T, weight_grad
 
 

time: 79.4 us -> 73.4 us (0.924)
  local copies, waits for them, and re-layouts: 2.99 us -> 0 us
  Pallas kernels: 74.8 us -> 71.9 us
    pallas_call x1, Pallas kernels: 74.8 us -> 70.3 us  [on_device(): pl.pallas_call(kernel, out_shape=(jax.ShapeDtypeStruct((WIDTH, rows), BF1...]
    unnamed x2 -> x0, local copies, waits for them, and re-layouts: 2.99 us -> none
    pallas_call x0 -> x1, Pallas kernels: none -> 1.62 us  [on_device(): pl.pallas_call(hand_out, out_shape=(jax.ShapeDtypeStruct(hidden.shape, BF...]
where the time goes in v3:
time: 73.4 us; the launch traced here: 73.2 us
  Pallas kernels  71.9 us (98%)
  between operations  1.28 us (2%)
    pallas_call x1, Pallas kernels, on_device(): pl.pallas_call(kernel, out_shape=(jax.ShapeDtypeStruct((WIDTH, rows), BF1...  70.3 us
    pallas_call x1, Pallas kernels, on_device(): pl.pallas_call(hand_out, out_shape=(jax.ShapeDtypeStruct(hidden.shape, BF...  1.62 us

profile of v3, /device:TPU:1, one launch (start us, length us, event | category | flops | bytes accessed | tf_op | source)
XLA Modules:
  0.0 73.2 jit_solution(18286173721308226747)
XLA Ops:
  1.3 70.3 %shard_map.59 = (bf16[96,1024]{1,0:T(8,128)(2,1)}, f32[2,32,96]{2,1,0:T(8,128)}) custom-call(bf16[1024,4096]{1,0:T(8,128)(2,1)} %tok_hbm.1, bf16[96,1024]{1,0:T(8,128)(2,1)} %bitcast.2, f32[2,32,96]{2,1,0:T(8,128)} %master_hbm.1, s32[1]{0:T(128)S(6)} %copy.6.counts_hbm), custom_call_target="tpu_custom_call" | custom-call | tf_op jit(solution)/shard_map/pallas_call | solution.py:387
  71.5 1.6 %shard_map.60 = (bf16[96,1024]{1,0:T(8,128)(2,1)}, f32[2,32,96]{2,1,0:T(8,128)}) custom-call(bf16[96,1024]{1,0:T(8,128)(2,1)} %get-tuple-element.6.hidden_in, f32[2,32,96]{2,1,0:T(8,128)} %get-tuple-element.7.grad_in), custom_call_target="tpu_custom_call" | custom-call | tf_op jit(solution)/shard_map/pallas_call | solution.py:429

commit v4 on v3

--- a/solution.py
+++ b/solution.py
@@ -12,6 +12,8 @@
 NZ, NY = 8, 8
 ROWS, WIDTH = 32, 96
 PACKED = 48
+FAR_OUT = (3,)
+FAR_IN = (3,)
 
 
 def pack(block):
@@ -23,10 +25,10 @@
     tok_hbm, hgT_hbm, master_hbm, counts_hbm,
     hidT_hbm, wg_ref,
     master_ref, counts_ref, tok, tokT, hgT, wbuf, w_y, acc, cotT, hidT, cnt,
-    part, xsend, xrecv, rsend, rrecv, own, zsend, zrecv,
+    part, xsend, xrecv, rsend, rrecv, dsend, drecv, own, zsend, zrecv,
     tok_sem, hg_sem, hid_sem, small_sem,
     cx_s, cx_r, ch_s, ch_r, az_u, az_d, az_r, ay_s, ay_r, ac_s, ac_r,
-    rc_s, rc_r, ry_s, ry_r, rz_s, rz_r,
+    rc_s, rc_r, ry_s, ry_r, rz_s, rz_r, ad_s, ad_r, rd_s, rd_r,
 ):
     node, loc = lax.axis_index("node"), lax.axis_index("local")
     z, y, c = node // (2 * NY), (node // 2) % NY, node % 2
@@ -183,6 +185,11 @@
         else:
             acc[...] += d
 
+    def ad(offset, k):
+        block = wbuf.at[c, y, pair(k)]
+        i = offset % NY
+        return remote(block, block, ad_s.at[i, k], ad_r.at[i, k], at(z, ring(offset), c))
+
     def gather(k, s):
         if s == 0:
             for i in range(2):
@@ -192,9 +199,18 @@
                 def _():
                     az_wait(origin)
 
-            for d in range(2):
-                push(ay(d, 1, k))
+            if k in FAR_OUT:
+                for offset in (3, -3, 2, -2, 1, -1):
+                    push(ad(offset, k))
+            else:
+                for d in range(2):
+                    push(ay(d, 1, k))
             push(ac(0, k, c))
+            return
+        if k in FAR_OUT:
+            for offset in (4,) if s == 4 else (s, -s):
+                ad(offset, k).wait_recv()
+                push(ac(-offset if s < 4 else 4, k, c))
             return
         for d in range(2):
             if s == 4 and d != k % 2:
@@ -224,6 +240,9 @@
         for k in range(4):
             if 0 <= t - k <= 4:
                 gather(k, t - k)
+            if t == 4 and k == 0:
+                for far in FAR_OUT:
+                    push(ad(4, far))
         if t == 0:
             pass_up(2)
         for i in ([0], [1, 2], [3, 4], [5, 6, 7], [], [], [], [])[t]:
@@ -275,6 +294,16 @@
         i = offset % NY
         rc(offset).wait_recv()
         own[i] = pack(part[i, :, c]) + xrecv[i].astype(F32)
+        if i:
+            for k in FAR_IN:
+                dsend[i, pair(k)] = own[i, pair(k)].astype(BF16)
+                push(rd(offset, k))
+
+    def rd(offset, k):
+        i = offset % NY
+        return remote(
+            dsend.at[i, pair(k)], drecv.at[i, pair(k)], rd_s.at[i, k], rd_r.at[i, k], at(z, ring(offset), c)
+        )
 
     def ry(d, s, k):
         return remote(
@@ -284,6 +313,8 @@
 
     def ry_send(s):
         for k in range(3, -1, -1):
+            if k in FAR_IN:
+                continue
             for d in range(2):
                 if s == 1 and d != k % 2:
                     continue
@@ -321,9 +352,14 @@
 
     for k in range(3, -1, -1):
         total = own[0, pair(k)]
-        for d in range(2):
-            ry(d, 4, k).wait_recv()
-            total = total + rrecv[d, 3, pair(k)].astype(F32)
+        if k in FAR_IN:
+            for offset in (4, 3, -3, 2, -2, 1, -1):
+                rd(offset, k).wait_recv()
+                total = total + drecv[offset % NY, pair(k)].astype(F32)
+        else:
+            for d in range(2):
+                ry(d, 4, k).wait_recv()
+                total = total + rrecv[d, 3, pair(k)].astype(F32)
         own[0, pair(k)] = total
         zsend[pair(k)] = total.astype(BF16)
         for i in range(2):
@@ -414,6 +450,8 @@
             vmem((NY, NZ, PACKED, 128), BF16),
             vmem((2, 4, NZ, PACKED, 128), BF16),
             vmem((2, 4, NZ, PACKED, 128), BF16),
+            vmem((NY, NZ, PACKED, 128), BF16),
+            vmem((NY, NZ, PACKED, 128), BF16),
             vmem((NY, NZ, PACKED, 128), F32),
             vmem((NZ, PACKED, 128), BF16),
             vmem((NZ, PACKED, 128), BF16),
@@ -421,6 +459,7 @@
             dma((3,)), dma((3,)), dma, dma, dma((4, 5)), dma((NZ,)), dma((NZ,)),
             dma((2, 4, 4)), dma((2, 4, 4)), dma((NY, 4)), dma((NY, 4)),
             dma((NY,)), dma((NY,)), dma((2, 4, 4)), dma((2, 4, 4)), dma((NZ,)), dma((NZ,)),
+            dma((NY, 4)), dma((NY, 4)), dma((NY, 4)), dma((NY, 4)),
         ],
         compiler_params=pltpu.CompilerParams(
             collective_id=1, has_side_effects=True, vmem_limit_bytes=56 * 2**20

time: 73.4 us -> 73.5 us (level)
  no operation moved by 1% of the time
where the time goes in v4:
time: 73.5 us; the launch traced here: 72.7 us
  Pallas kernels  71.5 us (97%)
  between operations  1.28 us (2%)
    pallas_call x1, Pallas kernels, on_device(): pl.pallas_call(kernel, out_shape=(jax.ShapeDtypeStruct((WIDTH, rows), BF1...  69.8 us
    pallas_call x1, Pallas kernels, on_device(): pl.pallas_call(hand_out, out_shape=(jax.ShapeDtypeStruct(hidden.shape, BF...  1.62 us

profile of v4, /device:TPU:1, one launch (start us, length us, event | category | flops | bytes accessed | tf_op | source)
XLA Modules:
  0.0 72.7 jit_solution(1117628538458064894)
XLA Ops:
  1.3 69.8 %shard_map.59 = (bf16[96,1024]{1,0:T(8,128)(2,1)}, f32[2,32,96]{2,1,0:T(8,128)}) custom-call(bf16[1024,4096]{1,0:T(8,128)(2,1)} %tok_hbm.1, bf16[96,1024]{1,0:T(8,128)(2,1)} %bitcast.2, f32[2,32,96]{2,1,0:T(8,128)} %master_hbm.1, s32[1]{0:T(128)S(6)} %copy.6.counts_hbm), custom_call_target="tpu_custom_call" | custom-call | tf_op jit(solution)/shard_map/pallas_call | solution.py:423
  71.1 1.6 %shard_map.60 = (bf16[96,1024]{1,0:T(8,128)(2,1)}, f32[2,32,96]{2,1,0:T(8,128)}) custom-call(bf16[96,1024]{1,0:T(8,128)(2,1)} %get-tuple-element.6.hidden_in, f32[2,32,96]{2,1,0:T(8,128)} %get-tuple-element.7.grad_in), custom_call_target="tpu_custom_call" | custom-call | tf_op jit(solution)/shard_map/pallas_call | solution.py:468
